TPU v7x, 512 devices: a whole 4x4x16 slice. The times are simulated.
512 devices in a mesh: site: 32 (over z, core), sector: 16 (over y, x).
Axes of the slice: x: 4, y: 4, z: 16, core: 2. Of those that a mesh axis runs over, the one named last changes fastest.
Arguments:
- site_tensors: bfloat16 [64, 32, 4, 128, 128], P('site', 'sector'), may hold values from -0.375 to 0.375
- charge_step: int32 [64, 4], P('site'), may hold values from -2 to 2, as said below
- local_operator: bfloat16 [13, 13, 4], replicated, may hold values from -1.75 to 1.75
- left_boundary: bfloat16 [32, 32, 13, 128, 128], P('site', 'sector'), may hold values from -6 to 6
- right_boundary: bfloat16 [32, 32, 13, 128, 128], P('site', 'sector'), may hold values from -6 to 6
Outputs:
- new_left: bfloat16 [32, 32, 13, 128, 128], P('site', 'sector')
- new_right: bfloat16 [32, 32, 13, 128, 128], P('site', 'sector')
Inputs may be any that keep to these rules, and one draw needn't show every extreme that they name: `charge_step`: at every site one local state shifts the sector label by 2 and another by -2.
All inputs are finite; a program needn't handle non-finite values.
Results may differ from a plain program's by a relative error of at most 0.011.
Values may be sent and summed in bfloat16 or wider, within the bound.
A program may use at most 64 MiB of HBM per device.

v0:
```python
import functools

import jax
import jax.numpy as jnp
from jax import lax
from jax.experimental import pallas as pl
from jax.experimental.pallas import tpu as pltpu
from jax.sharding import PartitionSpec as P

MESH = pl.DeviceIdType.MESH
BF = jnp.bfloat16
F32 = jnp.float32
W = 13
S = 4
BS = 128
R = 16
KW = W * R


def dot(a, b):
    return jnp.dot(a, b, preferred_element_type=F32)


def dot_nt(a, b):
    return lax.dot_general(a, b, (((1,), (1,)), ((), ())), preferred_element_type=F32)


def kernel(
    zs, steps_in, op_ref, m_in, left_in, right_in, left_out, right_out,
    tens, win1, win2, land, shr, res, own, prod, mix, kron, mt, steps_v, steps_s,
    st_send, st_recv, m_send, m_recv, e_send, e_recv, x_send, x_recv, o_send, o_recv, loc,
):
    site = lax.axis_index("site")
    sector = lax.axis_index("sector")
    z, c = site // 2, site % 2
    y, x = sector // 4, sector % 4
    half = x // 2
    slot = x % 2
    home = half == c
    is_right = (x == 0) | (x == 3)
    is_left = jnp.logical_not(is_right)

    def dev(zz, cc, yy, xx):
        return (zz * 2 + cc, yy * 4 + xx)

    def signal(sem, target):
        pl.semaphore_signal(sem, inc=1, device_id=target, device_id_type=MESH)

    left_task = dev(z, half, y, 1 + c)
    right_task = dev(z, half, y, 3 * c)
    left_next = dev(z + c, half, y, 2 - c)
    right_next = dev(z + c - 1, half, y, 3 - 3 * c)
    has_left_next = z + c < zs
    has_right_next = z + c - 1 >= 0
    src = [dev(z, half, y, 2 * c + k) for k in range(2)]
    away = half - 1 + is_right.astype(jnp.int32)
    fed = (z + away >= 0) & (z + away < zs)
    env_src = [dev(z + away, 1 - half, y, 2 * c + k) for k in range(2)]
    down = dev(z, 1 - c, (y + c + 3) % 4, x)
    up = dev(z, 1 - c, (y + c) % 4, x)

    barrier = pltpu.get_barrier_semaphore()
    for k in range(2):
        pl.when(jnp.logical_not(home & (slot == k)))(functools.partial(signal, barrier, src[k]))
        pl.when(fed)(functools.partial(signal, barrier, env_src[k]))
    pl.when(x != 1 + c)(functools.partial(signal, barrier, left_task))
    pl.when(x != 3 * c)(functools.partial(signal, barrier, right_task))
    signal(barrier, down)
    signal(barrier, up)
    pl.semaphore_wait(
        barrier,
        6
        - 2 * home.astype(jnp.int32)
        + has_left_next.astype(jnp.int32)
        + has_right_next.astype(jnp.int32),
    )

    def remote(a, b, ss, rs, target):
        return pltpu.make_async_remote_copy(
            src_ref=a, dst_ref=b, send_sem=ss, recv_sem=rs, device_id=target, device_id_type=MESH
        )

    def push(a, b, ss, rs, target, here):
        @pl.when(here)
        def _():
            pltpu.make_async_copy(a, b, rs).start()

        @pl.when(jnp.logical_not(here))
        def _():
            remote(a, b, ss, rs, target).start()

    def pushed(a, b, ss, rs, target, here):
        @pl.when(jnp.logical_not(here))
        def _():
            remote(a, b, ss, rs, target).wait_send()

    def arrived(b, rs):
        pltpu.make_async_copy(b, b, rs).wait()

    tasks = ((left_task, x == 1 + c), (right_task, x == 3 * c))

    def steps_args(t):
        return (steps_in, steps_v.at[slot], st_send.at[t], st_recv.at[slot]) + tasks[t]

    def m_args(t, k):
        return (
            m_in.at[k], tens.at[k, pl.ds(2 * slot, 2)], m_send.at[t, k], m_recv.at[k, slot]
        ) + tasks[t]

    def env_copy(t):
        held, target = ((left_in, left_next), (right_in, right_next))[t]
        return remote(
            held.at[0], win1.at[pl.ds(2 + 2 * slot, 2)], e_send.at[t], e_recv.at[slot], target
        )

    has_next = (has_left_next, has_right_next)
    for t in range(2):
        push(*steps_args(t))
    for t in range(2):
        push(*m_args(t, t))
        pl.when(has_next[t])(lambda t=t: env_copy(t).start())
    for t in range(2):
        push(*m_args(t, 1 - t))

    @pl.when(jnp.logical_not(fed))
    def _():
        win1[2:6] = jnp.zeros((4, W, BS, BS), BF)

    rows = lax.broadcasted_iota(jnp.int32, (KW, R), 0)
    cols = lax.broadcasted_iota(jnp.int32, (KW, R), 1)
    spread = (rows // R == cols).astype(F32).astype(BF)
    by_row = dot(spread, op_ref[...]).astype(BF)
    rows = lax.broadcasted_iota(jnp.int32, (KW, BS), 0)
    cols = lax.broadcasted_iota(jnp.int32, (KW, BS), 1)
    place_row = lax.broadcasted_iota(jnp.int32, (KW, KW), 0) % R
    place_col = lax.broadcasted_iota(jnp.int32, (KW, KW), 1) % R
    for s in range(S):
        pick = ((rows // R) * S + s == cols).astype(F32).astype(BF)

        @pl.when(is_left)
        def _():
            full = dot_nt(pick, by_row)
            kron[s] = jnp.where(place_row == place_col, full, 0.0).astype(BF)

        @pl.when(is_right)
        def _():
            full = dot_nt(by_row, pick)
            kron[s] = jnp.where(place_row == place_col, full, 0.0).astype(BF)

    for k in range(2):
        arrived(steps_v.at[k], st_recv.at[k])
    fetch = pltpu.make_async_copy(steps_v.at[0], steps_s, loc)
    fetch.start()
    fetch.wait()

    outer = c
    inner = 1 - c

    def wait_env(g):
        @pl.when(fed)
        def _():
            arrived(win1.at[pl.ds(2 + 2 * g, 2)], e_recv.at[g])

    def wait_m(k, g):
        arrived(tens.at[k, pl.ds(2 * g, 2)], m_recv.at[k, g])

    def swap_send(a, k, g):
        @pl.when(g == 0)
        def _():
            remote(a, land.at[k, 1], x_send.at[k, 0], x_recv.at[k, 1], down).start()

        @pl.when(g == 1)
        def _():
            remote(a, land.at[k, 0], x_send.at[k, 1], x_recv.at[k, 0], up).start()

    def wait_land(k, g):
        arrived(land.at[k, g], x_recv.at[k, g])

    def out_args(g, target_ref, t):
        here = home & (slot == g)
        return (
            res.at[pl.ds(2 * g, 2)], target_ref.at[0], o_send.at[g], o_recv.at[t],
            dev(z, half, y, 2 * c + g), here,
        )

    def blend(load, store):
        for s in range(S):
            for a in range(0, BS // R, 2):
                both = jnp.concatenate([load(s, a), load(s, a + 1)], axis=1)
                r = dot(kron[s], both).astype(BF)
                store(s, a, r[:, :BS].reshape(W, R, BS))
                store(s, a + 1, r[:, BS:].reshape(W, R, BS))

    @pl.when(is_left)
    def _():
        mt[4] = jnp.zeros((S, BS, BS), BF)

        def flip(k, g):
            def body(n, carry):
                i = 2 * g + n
                for s in range(S):
                    mt[i, s] = tens[k, i, s].astype(F32).T.astype(BF)
                return carry

            lax.fori_loop(0, 2, body, 0)

        def expand(k, win, g):
            def body(n, carry):
                i = 2 * g + n
                for p in range(2):
                    m = jnp.concatenate([tens[k, i, 2 * p], tens[k, i, 2 * p + 1]], axis=1)
                    r = dot(win[2 + i].reshape(W * BS, BS), m).astype(BF)
                    prod[p] = r.reshape(W, BS, 2 * BS)

                def load(s, a):
                    block = prod[s // 2, :, a * R : (a + 1) * R, (s % 2) * BS : (s % 2 + 1) * BS]
                    return block.reshape(KW, BS)

                def store(s, a, r):
                    mix[i, s, :, a * R : (a + 1) * R, :] = r

                blend(load, store)
                return carry

            lax.fori_loop(0, 2, body, 0)

        def reach(k, j, low, high, put):
            origin = [j - steps_s[k, s] for s in range(S)]
            inside = [(i >= low) & (i <= high) for i in origin]
            clipped = [jnp.minimum(jnp.maximum(i, low), high) for i in origin]
            lhs = jnp.concatenate(
                [mt[jnp.where(inside[s], clipped[s], 4), s] for s in range(S)], axis=1
            )
            for v0 in range(0, W, 2):
                vs = range(v0, min(v0 + 2, W))
                rhs = jnp.concatenate(
                    [
                        jnp.concatenate([mix[clipped[s], s, v] for s in range(S)], axis=0)
                        for v in vs
                    ],
                    axis=1,
                )
                r = dot(lhs, rhs).astype(BF)
                for n, v in enumerate(vs):
                    put(v, r[:, n * BS : (n + 1) * BS])

        def share(k, g):
            def body(n, carry):
                def put(v, r):
                    shr[k, g, n, v] = r

                reach(k, 6 * g - 2 + n, 2 * g, 2 * g + 1, put)
                return carry

            lax.fori_loop(0, 2, body, 0)
            swap_send(shr.at[k, g], k, g)

        def settle(k):
            def body(j, carry):
                def put(v, r):
                    own[j, v] = r

                reach(k, j, 0, 3, put)
                return carry

            lax.fori_loop(0, 4, body, 0)

        def join(k, g, put):
            wait_land(k, g)

            def body(n, carry):
                j = 2 * g + n
                put(j, (own[j].astype(F32) + land[k, g, n].astype(F32)).astype(BF))
                return carry

            lax.fori_loop(0, 2, body, 0)

        def put_mid(j, r):
            win2[2 + j] = r

        def put_res(j, r):
            res[j] = r

        for g in (outer, inner):
            wait_m(0, g)
            flip(0, g)
            wait_env(g)
            expand(0, win1, g)
            share(0, g)
        settle(0)
        for g in (inner, outer):
            wait_m(1, g)
            flip(1, g)
            join(0, g, put_mid)
            expand(1, win2, g)
            share(1, g)
        settle(1)
        for g in (inner, outer):
            join(1, g, put_res)
            push(*out_args(g, left_out, 0))
        for g in (inner, outer):
            pushed(*out_args(g, left_out, 0))
        for k in range(2):
            for g in range(2):
                remote(
                    shr.at[k, g], land.at[k, 1 - g], x_send.at[k, g], x_recv.at[k, 1 - g], up
                ).wait_send()

    @pl.when(is_right)
    def _():
        def widen(k, win, g):
            wait_land(k, g)
            win[pl.ds(6 * g, 2)] = land[k, g]

        def update(k, win, g, put):
            def body(n, carry):
                i = 2 * g + n
                at = [2 + i + steps_s[k, s] for s in range(S)]

                def load(s, a):
                    return win[at[s], :, a * R : (a + 1) * R, :].reshape(KW, BS)

                def store(s, a, r):
                    mix[0, s, :, a * R : (a + 1) * R, :] = r

                blend(load, store)
                for s in range(S):
                    for w0 in range(0, W, 2):
                        ws = range(w0, min(w0 + 2, W))
                        rhs = jnp.concatenate([mix[0, s, w] for w in ws], axis=1)
                        r = dot(tens[k, i, s], rhs).astype(BF)
                        for m, w in enumerate(ws):
                            prod[s // 2, w, :, (s % 2) * BS : (s % 2 + 1) * BS] = r[
                                :, m * BS : (m + 1) * BS
                            ]
                rhs = jnp.concatenate([tens[k, i, s] for s in range(S)], axis=1)
                for w in range(W):
                    lhs = jnp.concatenate([prod[0, w], prod[1, w]], axis=1)
                    put(i, w, dot_nt(lhs, rhs).astype(BF))
                return carry

            lax.fori_loop(0, 2, body, 0)

        def put_mid(i, w, r):
            win2[2 + i, w] = r

        def put_res(i, w, r):
            res[i, w] = r

        for g in (outer, inner):
            wait_env(g)
            swap_send(win1.at[pl.ds(2 + 2 * g, 2)], 0, g)
        for g in (inner, outer):
            wait_m(1, g)
            widen(0, win1, g)
            update(1, win1, g, put_mid)
            swap_send(win2.at[pl.ds(2 + 2 * g, 2)], 1, g)
        for g in (inner, outer):
            wait_m(0, g)
            widen(1, win2, g)
            update(0, win2, g, put_res)
            push(*out_args(g, right_out, 1))
        for g in (inner, outer):
            pushed(*out_args(g, right_out, 1))
        for k, win in ((0, win1), (1, win2)):
            for g in range(2):
                remote(
                    win.at[pl.ds(2 + 2 * g, 2)], land.at[k, 1 - g], x_send.at[k, g],
                    x_recv.at[k, 1 - g], up,
                ).wait_send()

    for t in range(2):
        pushed(*steps_args(t))
        pl.when(has_next[t])(lambda t=t: env_copy(t).wait_send())
        for k in range(2):
            pushed(*m_args(t, k))
    arrived(left_out.at[0], o_recv.at[0])
    arrived(right_out.at[0], o_recv.at[1])


def solution(mesh):
    zs = mesh.shape["site"] // 2

    def shards(site_tensors, charge_step, local_operator, left_boundary, right_boundary):
        steps = jnp.zeros((8, BS), jnp.int32).at[:2, :S].set(charge_step)
        op = jnp.zeros((R, BS), BF).at[:W, : W * S].set(local_operator.reshape(W, W * S))
        vmem = pl.BlockSpec(memory_space=pltpu.VMEM)
        anywhere = pl.BlockSpec(memory_space=pl.ANY)
        dma = pltpu.SemaphoreType.DMA
        env = (W, BS, BS)
        return pl.pallas_call(
            functools.partial(kernel, zs),
            out_shape=(
                jax.ShapeDtypeStruct(left_boundary.shape, BF),
                jax.ShapeDtypeStruct(right_boundary.shape, BF),
            ),
            in_specs=[vmem, vmem, anywhere, anywhere, anywhere],
            out_specs=(anywhere, anywhere),
            scratch_shapes=[
                pltpu.VMEM((2, 4, S, BS, BS), BF),
                pltpu.VMEM((8,) + env, BF),
                pltpu.VMEM((8,) + env, BF),
                pltpu.VMEM((2, 2, 2) + env, BF),
                pltpu.VMEM((2, 2, 2) + env, BF),
                pltpu.VMEM((4,) + env, BF),
                pltpu.VMEM((4,) + env, BF),
                pltpu.VMEM((2, W, BS, 2 * BS), BF),
                pltpu.VMEM((4, S) + env, BF),
                pltpu.VMEM((S, KW, KW), BF),
                pltpu.VMEM((5, S, BS, BS), BF),
                pltpu.VMEM((2, 8, BS), jnp.int32),
                pltpu.SMEM((8, BS), jnp.int32),
                dma((2,)),
                dma((2,)),
                dma((2, 2)),
                dma((2, 2)),
                dma((2,)),
                dma((2,)),
                dma((2, 2)),
                dma((2, 2)),
                dma((2,)),
                dma((2,)),
                dma,
            ],
            compiler_params=pltpu.CompilerParams(
                collective_id=0, has_side_effects=True, vmem_limit_bytes=52 * 2**20
            ),
        )(steps, op, site_tensors, left_boundary, right_boundary)

    placed = (
        P("site", "sector", None, None, None),
        P("site", None),
        P(),
        P("site", "sector", None, None, None),
        P("site", "sector", None, None, None),
    )
    return jax.shard_map(
        shards,
        mesh=mesh,
        in_specs=placed,
        out_specs=(P("site", "sector", None, None, None), P("site", "sector", None, None, None)),
        check_vma=False,
    )
```

profile of v0, /device:TPU:481, one launch (start us, length us, event | category | flops | bytes accessed | tf_op | source)
XLA Modules:
  0.0 101.8 jit_solution(10743800718285551605)
XLA Ops:
  0.6 0.7 scatter.6.steps_in
  1.3 0.8 copy.8
  2.2 0.1 copy.9
  2.3 0.0 copy-start
  2.3 1.0 %copy-done = bf16[2,2,4,128,128]{4,3,2,1,0:T(8,128)(2,1)S(1)} copy-done((bf16[2,2,4,128,128]{4,3,2,1,0:T(8,128)(2,1)S(1)}, bf16[2,2,4,128,128]{4,3,2,1,0:T(8,128)(2,1)}, u32[]{:S(2)}) %copy-start) | copy-done | bytes 524312
  3.3 96.1 %shard_map.68 = (bf16[1,2,13,128,128]{4,3,2,1,0:T(8,128)(2,1)S(1)}, bf16[1,2,13,128,128]{4,3,2,1,0:T(8,128)(2,1)}) custom-call(s32[8,128]{1,0:T(8,128)S(1)} %scatter.6.steps_in, bf16[16,128]{1,0:T(8,128)(2,1)S(1)} %scatter.9.op_ref, bf16[2,2,4,128,128]{4,3,2,1,0:T(8,128)(2,1)S(1)} %copy-done, bf16[1,2,13,128,128]{4,3,2,1,0:T(8,128)(2,1)} %left_in.1, ...), custom_call_target="tpu_custom_call" | custom-call | tf_op jit(solution)/shard_map/pallas_call | solution.py:391
  99.5 0.0 copy-start.1
  99.5 0.9 copy.12
  100.4 0.6 copy-done.1
  100.9 0.9 copy.13
  (2 shorter events, 0.0 us)
Async XLA Ops:
  2.3 1.1 %copy-start = (bf16[2,2,4,128,128]{4,3,2,1,0:T(8,128)(2,1)S(1)}, bf16[2,2,4,128,128]{4,3,2,1,0:T(8,128)(2,1)}, u32[]{:S(2)}) copy-start(bf16[2,2,4,128,128]{4,3,2,1,0:T(8,128)(2,1)} %m_in.1) | copy-start | bytes 1572868
  99.5 1.5 %copy-start.1 = (bf16[1,2,13,128,128]{4,3,2,1,0:T(8,128)(2,1)S(1)}, bf16[1,2,13,128,128]{4,3,2,1,0:T(8,128)(2,1)}, u32[]{:S(2)}) copy-start(bf16[1,2,13,128,128]{4,3,2,1,0:T(8,128)(2,1)} %get-tuple-element.29) | copy-start | bytes 2555908
where the time goes:
time: 102 us
  Pallas kernels  96.1 us (94%)
  local copies, waits for them, and re-layouts  5.03 us (5%)
    pallas_call x1, Pallas kernels, shards(): pl.pallas_call(functools.partial(kernel, zs), out_shape=(jax.ShapeDtypeSt...  96.1 us
    unnamed x7, local copies, waits for them, and re-layouts  4.23 us

commit v1 on v0

--- a/solution.py
+++ b/solution.py
@@ -27,8 +27,8 @@
 
 def kernel(
     zs, steps_in, op_ref, m_in, left_in, right_in, left_out, right_out,
-    tens, win1, win2, land, shr, res, own, prod, mix, kron, mt, steps_v, steps_s,
-    st_send, st_recv, m_send, m_recv, e_send, e_recv, x_send, x_recv, o_send, o_recv, loc,
+    tens, win1, win2, land, shr, res, own, relay, prod, mix, kron, mt, op_v, steps_h, steps_v, steps_s,
+    st_send, st_recv, m_send, m_recv, e_send, e_recv, r_send, r_recv, x_send, x_recv, o_send, o_recv, loc,
 ):
     site = lax.axis_index("site")
     sector = lax.axis_index("sector")
@@ -48,31 +48,46 @@
 
     left_task = dev(z, half, y, 1 + c)
     right_task = dev(z, half, y, 3 * c)
-    left_next = dev(z + c, half, y, 2 - c)
-    right_next = dev(z + c - 1, half, y, 3 - 3 * c)
-    has_left_next = z + c < zs
-    has_right_next = z + c - 1 >= 0
+    left_near, left_far = c == 0, (c == 1) & (z + 1 < zs)
+    right_near, right_far = c == 1, (c == 0) & (z >= 1)
+    left_next = dev(z, half, y, 2)
+    right_next = dev(z, half, y, 0)
+    left_step = dev(z + 1, half, y, x)
+    right_step = dev(z - 1, half, y, x)
+    left_via = home & (z >= 1)
+    right_via = home & (z + 1 < zs)
+    left_last = dev(z, half, y, 1)
+    right_last = dev(z, half, y, 3)
+    left_from = dev(z - 1, 1, y, x)
+    right_from = dev(z + 1, 0, y, x)
     src = [dev(z, half, y, 2 * c + k) for k in range(2)]
     away = half - 1 + is_right.astype(jnp.int32)
     fed = (z + away >= 0) & (z + away < zs)
-    env_src = [dev(z + away, 1 - half, y, 2 * c + k) for k in range(2)]
+    near = away == 0
+    env_src = [dev(z, jnp.where(near, 1 - half, c), y, 2 * c + k) for k in range(2)]
     down = dev(z, 1 - c, (y + c + 3) % 4, x)
     up = dev(z, 1 - c, (y + c) % 4, x)
+
+    steps_h[...] = jnp.zeros((8, BS), jnp.int32)
+    steps_h[0:2, 0:S] = steps_in[...]
 
     barrier = pltpu.get_barrier_semaphore()
     for k in range(2):
         pl.when(jnp.logical_not(home & (slot == k)))(functools.partial(signal, barrier, src[k]))
-        pl.when(fed)(functools.partial(signal, barrier, env_src[k]))
+        pl.when(fed & (near | (x != 2 * c + k)))(functools.partial(signal, barrier, env_src[k]))
     pl.when(x != 1 + c)(functools.partial(signal, barrier, left_task))
     pl.when(x != 3 * c)(functools.partial(signal, barrier, right_task))
+    pl.when(left_via)(functools.partial(signal, barrier, left_from))
+    pl.when(right_via)(functools.partial(signal, barrier, right_from))
     signal(barrier, down)
     signal(barrier, up)
     pl.semaphore_wait(
         barrier,
-        6
+        7
         - 2 * home.astype(jnp.int32)
-        + has_left_next.astype(jnp.int32)
-        + has_right_next.astype(jnp.int32),
+        + (left_far | right_far).astype(jnp.int32)
+        + (left_via & (x != 1)).astype(jnp.int32)
+        + (right_via & (x != 3)).astype(jnp.int32),
     )
 
     def remote(a, b, ss, rs, target):
@@ -100,51 +115,74 @@
     tasks = ((left_task, x == 1 + c), (right_task, x == 3 * c))
 
     def steps_args(t):
-        return (steps_in, steps_v.at[slot], st_send.at[t], st_recv.at[slot]) + tasks[t]
+        return (steps_h, steps_v.at[slot], st_send.at[t], st_recv.at[slot]) + tasks[t]
 
     def m_args(t, k):
         return (
             m_in.at[k], tens.at[k, pl.ds(2 * slot, 2)], m_send.at[t, k], m_recv.at[k, slot]
         ) + tasks[t]
 
-    def env_copy(t):
+    def near_copy(t, n):
         held, target = ((left_in, left_next), (right_in, right_next))[t]
         return remote(
-            held.at[0], win1.at[pl.ds(2 + 2 * slot, 2)], e_send.at[t], e_recv.at[slot], target
+            held.at[0, n], win1.at[2 + 2 * slot + n], e_send.at[t, n], e_recv.at[slot, n], target
         )
 
-    has_next = (has_left_next, has_right_next)
+    def far_copy(t, n):
+        held, target = ((left_in, left_step), (right_in, right_step))[t]
+        return remote(
+            held.at[0, n], relay.at[t, n], e_send.at[t, n], r_recv.at[t, n], target
+        )
+
+    def via_args(t, n):
+        return (
+            relay.at[t, n], win1.at[2 + 2 * slot + n], r_send.at[t, n], e_recv.at[slot, n],
+            (left_last, right_last)[t], x == (1, 3)[t],
+        )
+
+    envs = ((left_near, left_far, left_via), (right_near, right_far, right_via))
+
+    def env_ends(t, n):
+        pl.when(envs[t][0])(lambda: near_copy(t, n).wait_send())
+        pl.when(envs[t][1])(lambda: far_copy(t, n).wait_send())
+        pl.when(envs[t][2])(lambda: pushed(*via_args(t, n)))
+
+    for n in range(2):
+        for t in range(2):
+            pl.when(envs[t][1])(lambda t=t, n=n: far_copy(t, n).start())
+            pl.when(envs[t][0] & is_right)(lambda t=t, n=n: near_copy(t, n).start())
     for t in range(2):
         push(*steps_args(t))
     for t in range(2):
         push(*m_args(t, t))
-        pl.when(has_next[t])(lambda t=t: env_copy(t).start())
-    for t in range(2):
-        push(*m_args(t, 1 - t))
 
     @pl.when(jnp.logical_not(fed))
     def _():
         win1[2:6] = jnp.zeros((4, W, BS, BS), BF)
 
-    rows = lax.broadcasted_iota(jnp.int32, (KW, R), 0)
-    cols = lax.broadcasted_iota(jnp.int32, (KW, R), 1)
-    spread = (rows // R == cols).astype(F32).astype(BF)
-    by_row = dot(spread, op_ref[...]).astype(BF)
+    op_v[...] = jnp.zeros((64, BS), F32)
+    for w in range(W):
+        op_v[S * w : S * w + S, 0:W] = op_ref[w].astype(F32)
+    terms = op_v[...].astype(BF)
     rows = lax.broadcasted_iota(jnp.int32, (KW, BS), 0)
     cols = lax.broadcasted_iota(jnp.int32, (KW, BS), 1)
+    spread = (rows // R == cols).astype(F32).astype(BF)
+    rows = lax.broadcasted_iota(jnp.int32, (KW, 64), 0)
+    cols = lax.broadcasted_iota(jnp.int32, (KW, 64), 1)
     place_row = lax.broadcasted_iota(jnp.int32, (KW, KW), 0) % R
     place_col = lax.broadcasted_iota(jnp.int32, (KW, KW), 1) % R
     for s in range(S):
         pick = ((rows // R) * S + s == cols).astype(F32).astype(BF)
+        by_row = dot(pick, terms).astype(BF)
 
         @pl.when(is_left)
         def _():
-            full = dot_nt(pick, by_row)
+            full = dot_nt(spread, by_row)
             kron[s] = jnp.where(place_row == place_col, full, 0.0).astype(BF)
 
         @pl.when(is_right)
         def _():
-            full = dot_nt(by_row, pick)
+            full = dot_nt(by_row, spread)
             kron[s] = jnp.where(place_row == place_col, full, 0.0).astype(BF)
 
     for k in range(2):
@@ -159,29 +197,59 @@
     def wait_env(g):
         @pl.when(fed)
         def _():
-            arrived(win1.at[pl.ds(2 + 2 * g, 2)], e_recv.at[g])
+            for n in range(2):
+                arrived(win1.at[2 + 2 * g + n], e_recv.at[g, n])
 
     def wait_m(k, g):
         arrived(tens.at[k, pl.ds(2 * g, 2)], m_recv.at[k, g])
 
-    def swap_send(a, k, g):
-        @pl.when(g == 0)
-        def _():
-            remote(a, land.at[k, 1], x_send.at[k, 0], x_recv.at[k, 1], down).start()
-
-        @pl.when(g == 1)
-        def _():
-            remote(a, land.at[k, 0], x_send.at[k, 1], x_recv.at[k, 0], up).start()
-
-    def wait_land(k, g):
-        arrived(land.at[k, g], x_recv.at[k, g])
-
-    def out_args(g, target_ref, t):
+    def swap_copy(a, k, g, n, target):
+        return remote(
+            a, land.at[k, 1 - g, n], x_send.at[k, g, n], x_recv.at[k, 1 - g, n], target
+        )
+
+    def swap_send(a, k, g, n):
+        pl.when(g == 0)(lambda: swap_copy(a, k, 0, n, down).start())
+        pl.when(g == 1)(lambda: swap_copy(a, k, 1, n, up).start())
+
+    def wait_land(k, g, n):
+        arrived(land.at[k, g, n], x_recv.at[k, g, n])
+
+    def out_args(g, n, target_ref, t):
         here = home & (slot == g)
         return (
-            res.at[pl.ds(2 * g, 2)], target_ref.at[0], o_send.at[g], o_recv.at[t],
+            res.at[2 * g + n], target_ref.at[0, n], o_send.at[g, n], o_recv.at[t, n],
             dev(z, half, y, 2 * c + g), here,
         )
+
+    def edge_first():
+        for n in range(2):
+            swap_send(win1.at[2 + 2 * outer + n], 0, outer, n)
+
+    @pl.when(x == 0)
+    def _():
+        wait_env(outer)
+        edge_first()
+
+    @pl.when(is_left)
+    def _():
+        for t in range(2):
+            pushed(*m_args(t, t))
+        for n in range(2):
+            for t in range(2):
+                pl.when(envs[t][0])(lambda t=t, n=n: near_copy(t, n).start())
+
+    for n in range(2):
+        for t in range(2):
+
+            @pl.when(envs[t][2])
+            def _():
+                arrived(relay.at[t, n], r_recv.at[t, n])
+                push(*via_args(t, n))
+
+    def later_tensors():
+        for t in range(2):
+            push(*m_args(t, 1 - t))
 
     def blend(load, store):
         for s in range(S):
@@ -245,15 +313,13 @@
                     put(v, r[:, n * BS : (n + 1) * BS])
 
         def share(k, g):
-            def body(n, carry):
+            for n in range(2):
+
                 def put(v, r):
                     shr[k, g, n, v] = r
 
                 reach(k, 6 * g - 2 + n, 2 * g, 2 * g + 1, put)
-                return carry
-
-            lax.fori_loop(0, 2, body, 0)
-            swap_send(shr.at[k, g], k, g)
+                swap_send(shr.at[k, g, n], k, g, n)
 
         def settle(k):
             def body(j, carry):
@@ -265,54 +331,55 @@
 
             lax.fori_loop(0, 4, body, 0)
 
-        def join(k, g, put):
-            wait_land(k, g)
-
-            def body(n, carry):
-                j = 2 * g + n
-                put(j, (own[j].astype(F32) + land[k, g, n].astype(F32)).astype(BF))
+        def join(k, g, n):
+            wait_land(k, g, n)
+            j = 2 * g + n
+
+            def body(v, carry):
+                r = (own[j, v].astype(F32) + land[k, g, n, v].astype(F32)).astype(BF)
+                if k == 0:
+                    win2[2 + j, v] = r
+                else:
+                    res[j, v] = r
                 return carry
 
-            lax.fori_loop(0, 2, body, 0)
-
-        def put_mid(j, r):
-            win2[2 + j] = r
-
-        def put_res(j, r):
-            res[j] = r
-
-        for g in (outer, inner):
+            lax.fori_loop(0, W, body, 0)
+
+        for first, g in ((True, outer), (False, inner)):
             wait_m(0, g)
             flip(0, g)
             wait_env(g)
             expand(0, win1, g)
+            if not first:
+                later_tensors()
             share(0, g)
         settle(0)
-        for g in (inner, outer):
+        for g in (outer, inner):
             wait_m(1, g)
             flip(1, g)
-            join(0, g, put_mid)
+            for n in range(2):
+                join(0, g, n)
             expand(1, win2, g)
             share(1, g)
         settle(1)
         for g in (inner, outer):
-            join(1, g, put_res)
-            push(*out_args(g, left_out, 0))
-        for g in (inner, outer):
-            pushed(*out_args(g, left_out, 0))
-        for k in range(2):
-            for g in range(2):
-                remote(
-                    shr.at[k, g], land.at[k, 1 - g], x_send.at[k, g], x_recv.at[k, 1 - g], up
-                ).wait_send()
+            for n in range(2):
+                join(1, g, n)
+                push(*out_args(g, n, left_out, 0))
+        for g in range(2):
+            for n in range(2):
+                pushed(*out_args(g, n, left_out, 0))
+                for k in range(2):
+                    swap_copy(shr.at[k, g, n], k, g, n, up).wait_send()
 
     @pl.when(is_right)
     def _():
         def widen(k, win, g):
-            wait_land(k, g)
-            win[pl.ds(6 * g, 2)] = land[k, g]
-
-        def update(k, win, g, put):
+            for n in range(2):
+                wait_land(k, g, n)
+                win[6 * g + n] = land[k, g, n]
+
+        def update(k, win, g, n, put):
             def body(n, carry):
                 i = 2 * g + n
                 at = [2 + i + steps_s[k, s] for s in range(S)]
@@ -337,9 +404,8 @@
                 for w in range(W):
                     lhs = jnp.concatenate([prod[0, w], prod[1, w]], axis=1)
                     put(i, w, dot_nt(lhs, rhs).astype(BF))
-                return carry
-
-            lax.fori_loop(0, 2, body, 0)
+
+            body(n, 0)
 
         def put_mid(i, w, r):
             win2[2 + i, w] = r
@@ -347,43 +413,50 @@
         def put_res(i, w, r):
             res[i, w] = r
 
-        for g in (outer, inner):
-            wait_env(g)
-            swap_send(win1.at[pl.ds(2 + 2 * g, 2)], 0, g)
-        for g in (inner, outer):
+        @pl.when(x == 3)
+        def _():
+            wait_env(outer)
+            edge_first()
+
+        wait_env(inner)
+        for n in range(2):
+            swap_send(win1.at[2 + 2 * inner + n], 0, inner, n)
+        for first, g in ((True, outer), (False, inner)):
             wait_m(1, g)
+            if first:
+                later_tensors()
             widen(0, win1, g)
-            update(1, win1, g, put_mid)
-            swap_send(win2.at[pl.ds(2 + 2 * g, 2)], 1, g)
+            for n in range(2):
+                update(1, win1, g, n, put_mid)
+                swap_send(win2.at[2 + 2 * g + n], 1, g, n)
         for g in (inner, outer):
             wait_m(0, g)
             widen(1, win2, g)
-            update(0, win2, g, put_res)
-            push(*out_args(g, right_out, 1))
-        for g in (inner, outer):
-            pushed(*out_args(g, right_out, 1))
-        for k, win in ((0, win1), (1, win2)):
-            for g in range(2):
-                remote(
-                    win.at[pl.ds(2 + 2 * g, 2)], land.at[k, 1 - g], x_send.at[k, g],
-                    x_recv.at[k, 1 - g], up,
-                ).wait_send()
+            for n in range(2):
+                update(0, win2, g, n, put_res)
+                push(*out_args(g, n, right_out, 1))
+        for g in range(2):
+            for n in range(2):
+                pushed(*out_args(g, n, right_out, 1))
+                for k, win in ((0, win1), (1, win2)):
+                    swap_copy(win.at[2 + 2 * g + n], k, g, n, up).wait_send()
 
     for t in range(2):
         pushed(*steps_args(t))
-        pl.when(has_next[t])(lambda t=t: env_copy(t).wait_send())
-        for k in range(2):
-            pushed(*m_args(t, k))
-    arrived(left_out.at[0], o_recv.at[0])
-    arrived(right_out.at[0], o_recv.at[1])
+        pl.when(is_right)(lambda t=t: pushed(*m_args(t, t)))
+        pushed(*m_args(t, 1 - t))
+        for n in range(2):
+            env_ends(t, n)
+    for n in range(2):
+        arrived(left_out.at[0, n], o_recv.at[0, n])
+        arrived(right_out.at[0, n], o_recv.at[1, n])
 
 
 def solution(mesh):
     zs = mesh.shape["site"] // 2
 
     def shards(site_tensors, charge_step, local_operator, left_boundary, right_boundary):
-        steps = jnp.zeros((8, BS), jnp.int32).at[:2, :S].set(charge_step)
-        op = jnp.zeros((R, BS), BF).at[:W, : W * S].set(local_operator.reshape(W, W * S))
+        op = local_operator.transpose(0, 2, 1)
         vmem = pl.BlockSpec(memory_space=pltpu.VMEM)
         anywhere = pl.BlockSpec(memory_space=pl.ANY)
         dma = pltpu.SemaphoreType.DMA
@@ -404,28 +477,33 @@
                 pltpu.VMEM((2, 2, 2) + env, BF),
                 pltpu.VMEM((4,) + env, BF),
                 pltpu.VMEM((4,) + env, BF),
+                pltpu.VMEM((2, 2) + env, BF),
                 pltpu.VMEM((2, W, BS, 2 * BS), BF),
                 pltpu.VMEM((4, S) + env, BF),
                 pltpu.VMEM((S, KW, KW), BF),
                 pltpu.VMEM((5, S, BS, BS), BF),
+                pltpu.VMEM((64, BS), F32),
+                pltpu.VMEM((8, BS), jnp.int32),
                 pltpu.VMEM((2, 8, BS), jnp.int32),
                 pltpu.SMEM((8, BS), jnp.int32),
                 dma((2,)),
                 dma((2,)),
                 dma((2, 2)),
                 dma((2, 2)),
-                dma((2,)),
-                dma((2,)),
-                dma((2, 2)),
-                dma((2, 2)),
-                dma((2,)),
-                dma((2,)),
+                dma((2, 2)),
+                dma((2, 2)),
+                dma((2, 2)),
+                dma((2, 2)),
+                dma((2, 2, 2)),
+                dma((2, 2, 2)),
+                dma((2, 2)),
+                dma((2, 2)),
                 dma,
             ],
             compiler_params=pltpu.CompilerParams(
-                collective_id=0, has_side_effects=True, vmem_limit_bytes=52 * 2**20
+                collective_id=0, has_side_effects=True, vmem_limit_bytes=62 * 2**20
             ),
-        )(steps, op, site_tensors, left_boundary, right_boundary)
+        )(charge_step, op, site_tensors, left_boundary, right_boundary)
 
     placed = (
         P("site", "sector", None, None, None),

time: 102 us -> 83 us (0.81)
  the two profiles are of different devices: /device:TPU:481 before, /device:TPU:6 now
where the time goes in v1:
time: 83 us; the launch traced here: 82.8 us
  Pallas kernels  79 us (95%)
  local copies, waits for them, and re-layouts  3.13 us (4%)
    pallas_call x1, Pallas kernels, shards(): pl.pallas_call(functools.partial(kernel, zs), out_shape=(jax.ShapeDtypeSt...  79 us
    unnamed x4, local copies, waits for them, and re-layouts  3.13 us

profile of v1, /device:TPU:6, one launch (start us, length us, event | category | flops | bytes accessed | tf_op | source)
XLA Modules:
  0.0 82.8 jit_solution(7290831815758300749)
XLA Ops:
  0.6 79.0 %shard_map.68 = (bf16[1,2,13,128,128]{4,3,2,1,0:T(8,128)(2,1)}, bf16[1,2,13,128,128]{4,3,2,1,0:T(8,128)(2,1)}) custom-call(s32[2,4]{1,0:T(2,128)} %steps_in.1, bf16[13,4,13]{2,1,0:T(4,128)(2,1)} %bitcast.1, bf16[2,2,4,128,128]{4,3,2,1,0:T(8,128)(2,1)} %m_in.1, bf16[1,2,13,128,128]{4,3,2,1,0:T(8,128)(2,1)} %left_in.1, bf16[1,2,13,128,128]{4,3,2,1,0:T(8,128)(2,1)} %right_in.1), custom_call_target="tpu_custom_call" | custom-call | tf_op jit(solution)/shard_map/pallas_call | solution.py:464
  79.6 0.0 copy-start
  79.6 2.2 %copy.9 = bf16[1,2,13,128,128]{4,3,2,1,0:T(8,128)(2,1)} copy(bf16[1,2,13,128,128]{4,3,2,1,0:T(8,128)(2,1)} %get-tuple-element.4) | data formatting | bytes 1703936
  81.9 0.0 copy-done
  81.9 0.9 %copy.10 = bf16[1,2,13,128,128]{4,3,2,1,0:T(8,128)(2,1)} copy(bf16[1,2,13,128,128]{4,3,2,1,0:T(8,128)(2,1)S(1)} %copy-done) | data formatting | bytes 1703936
Async XLA Ops:
  79.6 2.2 %copy-start = (bf16[1,2,13,128,128]{4,3,2,1,0:T(8,128)(2,1)S(1)}, bf16[1,2,13,128,128]{4,3,2,1,0:T(8,128)(2,1)}, u32[]{:S(2)}) copy-start(bf16[1,2,13,128,128]{4,3,2,1,0:T(8,128)(2,1)} %get-tuple-element.5) | copy-start | bytes 2555908

commit v2 on v1

--- a/solution.py
+++ b/solution.py
@@ -350,9 +350,9 @@
             flip(0, g)
             wait_env(g)
             expand(0, win1, g)
-            if not first:
+            share(0, g)
+            if first:
                 later_tensors()
-            share(0, g)
         settle(0)
         for g in (outer, inner):
             wait_m(1, g)

time: 83 us -> 84.4 us (1.017); the launches traced: 82.8 us -> 82.8 us
  no operation moved by 1% of the time
where the time goes in v2:
time: 84.4 us; the launch traced here: 82.8 us
  Pallas kernels  79.1 us (94%)
  local copies, waits for them, and re-layouts  3.13 us (4%)
    pallas_call x1, Pallas kernels, shards(): pl.pallas_call(functools.partial(kernel, zs), out_shape=(jax.ShapeDtypeSt...  79.1 us
    unnamed x4, local copies, waits for them, and re-layouts  3.13 us

profile of v2, /device:TPU:6, one launch (start us, length us, event | category | flops | bytes accessed | tf_op | source)
XLA Modules:
  0.0 82.8 jit_solution(7255685736653378923)
XLA Ops:
  0.6 79.1 %shard_map.68 = (bf16[1,2,13,128,128]{4,3,2,1,0:T(8,128)(2,1)}, bf16[1,2,13,128,128]{4,3,2,1,0:T(8,128)(2,1)}) custom-call(s32[2,4]{1,0:T(2,128)} %steps_in.1, bf16[13,4,13]{2,1,0:T(4,128)(2,1)} %bitcast.1, bf16[2,2,4,128,128]{4,3,2,1,0:T(8,128)(2,1)} %m_in.1, bf16[1,2,13,128,128]{4,3,2,1,0:T(8,128)(2,1)} %left_in.1, bf16[1,2,13,128,128]{4,3,2,1,0:T(8,128)(2,1)} %right_in.1), custom_call_target="tpu_custom_call" | custom-call | tf_op jit(solution)/shard_map/pallas_call | solution.py:464
  79.7 0.0 copy-start
  79.7 2.2 %copy.9 = bf16[1,2,13,128,128]{4,3,2,1,0:T(8,128)(2,1)} copy(bf16[1,2,13,128,128]{4,3,2,1,0:T(8,128)(2,1)} %get-tuple-element.4) | data formatting | bytes 1703936
  81.9 0.0 copy-done
  81.9 0.9 %copy.10 = bf16[1,2,13,128,128]{4,3,2,1,0:T(8,128)(2,1)} copy(bf16[1,2,13,128,128]{4,3,2,1,0:T(8,128)(2,1)S(1)} %copy-done) | data formatting | bytes 1703936
Async XLA Ops:
  79.7 2.2 %copy-start = (bf16[1,2,13,128,128]{4,3,2,1,0:T(8,128)(2,1)S(1)}, bf16[1,2,13,128,128]{4,3,2,1,0:T(8,128)(2,1)}, u32[]{:S(2)}) copy-start(bf16[1,2,13,128,128]{4,3,2,1,0:T(8,128)(2,1)} %get-tuple-element.5) | copy-start | bytes 2555908
